TPU v7x, 32 devices: a whole 2x2x4 slice. The times are simulated.
32 devices in a mesh: chan: 4 (over x, core), tm: 8 (over z, y).
Axes of the slice: x: 2, y: 2, z: 4, core: 2. Of those that a mesh axis runs over, the one named last changes fastest.
Arguments:
- record: float32 [2048, 65536], P('chan', 'tm'), may hold values from -6 to 6
- whitening: float32 [65], replicated, may hold values from -0.75 to 0.75
- offsets: int32 [128], P('tm'), may hold values from 0 to 256, as said below
- window_valid: int32 [128], P('tm'), may hold values 0 or 1
Outputs:
- cross_spectra: bfloat16 [64, 2, 2048, 2048], P('tm', None, 'chan')
Inputs may be any that keep to these rules, and one draw needn't show every extreme that they name: `offsets`: some window has offset exactly 256.
All inputs are finite; a program needn't handle non-finite values. No bound on the sum of `window_valid` on one device may be relied on, other than what follows from the above.
Results may differ from a plain program's by a relative error of at most 0.006.
Values may be sent and summed in bfloat16 or wider, within the bound.
No kernel may reach another device: no remote copies, remote signals or barrier semaphores. Data moves between devices by JAX's collectives and lax.ppermute only.
A program may use at most 192 MiB of HBM per device.

v0:
```python
import functools
import math

import jax
import jax.numpy as jnp
from jax import lax
from jax.experimental import pallas as pl
from jax.experimental.pallas import tpu as pltpu
from jax.sharding import PartitionSpec as P

L = 2048
HOP = 512
JITTER = 256
TAPS = 65
BINS = 64
K0 = 64
RIM = 128
GROUP = L // HOP
EDGE = RIM + JITTER
LANES = 2 * BINS
MIB = 1 << 20
F32 = jnp.float32
BF16 = jnp.bfloat16


def from_behind(shard, axis, by):
    devices = lax.axis_size(axis)
    pairs = [(i, i + by) for i in range(devices) if 0 <= i + by < devices]
    return lax.ppermute(shard, axis, pairs)


def matmul(a, b):
    return jnp.dot(a, b, preferred_element_type=F32)


def rotation(place):
    lane = lax.broadcasted_iota(jnp.int32, (8, LANES), 1)[:1]
    bins = K0 + (lane & (BINS - 1))
    angles = ((bins * place) & (L - 1)).astype(F32) * (2.0 * math.pi / L)
    sine = jnp.sin(angles)
    return jnp.cos(angles), jnp.where(lane < BINS, -sine, sine)


def turn(values, place):
    cosine, sine = rotation(jnp.full((8, LANES), place + L, jnp.int32))
    return values * cosine[:1] + pltpu.roll(values, BINS, 1) * sine[:1]


def edge_table(rise, fall, offset):
    start = JITTER - offset
    return jnp.concatenate([rise[pl.ds(start, RIM), :], fall[pl.ds(start, JITTER), :]], axis=0).astype(BF16)


def across(values):
    channels = values.shape[0]
    if channels % 128:
        values = jnp.pad(values, ((0, 128 - channels), (0, 0)))
    return values.T


def outbox_kernel(offsets, valid, whitening, record, out, taps):
    taps[...] = jnp.zeros_like(taps)
    for m in range(TAPS):
        taps[m : m + 1, :] = jnp.full((1, LANES), whitening[m], F32)
    top = record[0:8, :]
    row = lax.broadcasted_iota(jnp.int32, top.shape, 0)
    lane = lax.broadcasted_iota(jnp.int32, top.shape, 1)
    first = offsets.shape[0] - GROUP
    for q in range(GROUP):
        top = jnp.where((row == 0) & (lane == q), offsets[first + q].astype(F32), top)
        top = jnp.where((row == 0) & (lane == GROUP + q), valid[first + q].astype(F32), top)
    out[...] = jnp.concatenate([top, record[8:, :]], axis=0).astype(BF16)


def outbox(record, offsets, valid, whitening):
    channels, slab = record.shape
    smem = pl.BlockSpec(memory_space=pltpu.SMEM)
    return pl.pallas_call(
        outbox_kernel,
        grid=(1,),
        out_shape=(jax.ShapeDtypeStruct((channels, RIM), BF16), jax.ShapeDtypeStruct((TAPS + 7, LANES), F32)),
        in_specs=[smem, smem, smem, pl.BlockSpec((channels, RIM), lambda i: (0, slab // RIM - 1))],
        out_specs=(pl.BlockSpec(memory_space=pltpu.VMEM), pl.BlockSpec(memory_space=pltpu.VMEM)),
        compiler_params=pltpu.CompilerParams(vmem_limit_bytes=60 * MIB),
        name="outbox",
    )(offsets, valid, whitening, record)


def tables_kernel(taps, record, blocks, rise, fall, heads, sums, padded, lead, sem):
    fetch = pltpu.make_async_copy(record.at[:, pl.ds(0, lead.shape[1])], lead, sem)
    fetch.start()
    ramp_rows = TAPS - 1
    lane = lax.broadcasted_iota(jnp.int32, (8, LANES), 1)
    row = lax.broadcasted_iota(jnp.int32, (ramp_rows, LANES), 0)

    def phases(cosine, sine):
        half = lax.broadcasted_iota(jnp.int32, cosine.shape, 1) < BINS
        return jnp.where(half, cosine, sine * -1.0) * (1.0 / math.sqrt(L))

    first = phases(*rotation(row))
    padded[0:ramp_rows, :] = jnp.zeros((ramp_rows, LANES), F32)
    padded[ramp_rows : 2 * ramp_rows, :] = first
    padded[2 * ramp_rows :, :] = phases(*rotation(row[:8] + ramp_rows))
    ramp = jnp.zeros((ramp_rows, LANES), F32)
    gain = jnp.zeros((1, LANES), F32)
    for m in range(TAPS):
        tap = taps[m : m + 1, :]
        ramp = ramp + tap * padded[m : m + ramp_rows, :]
        gain = gain + tap * padded[ramp_rows + m : TAPS + m, :]
    gain = jnp.broadcast_to(gain * math.sqrt(L), (8, LANES))
    swapped = pltpu.roll(gain, BINS, 1)
    gain_re = jnp.where(lane < BINS, gain, swapped)[:1]
    gain_im = jnp.where(lane < BINS, -swapped, gain)[:1]
    cosine, sine = rotation(jnp.full((8, LANES), ramp_rows, jnp.int32))
    base = first * cosine[:1] + pltpu.roll(first, BINS, 1) * sine[:1]
    base = base * gain_re + pltpu.roll(base, BINS, 1) * gain_im
    other = pltpu.roll(base, BINS, 1)
    steps = L // ramp_rows
    onward = lax.broadcasted_iota(jnp.int32, (steps, LANES), 0)
    cosines, sines = rotation(L - onward * ramp_rows)
    ahead = JITTER // ramp_rows - 1
    for a in range(steps):
        pure = base * cosines[a : a + 1] + other * sines[a : a + 1]
        blocks[a * ramp_rows : (a + 1) * ramp_rows, :] = pure.astype(BF16)
        if a >= steps - ahead:
            at = (a - steps + ahead) * ramp_rows
            fall[at : at + ramp_rows, :] = pure
        if a == 0:
            fall[ahead * ramp_rows : JITTER, :] = pure - ramp
    fall[JITTER:, :] = jnp.zeros((fall.shape[0] - JITTER, LANES), F32)
    rise[...] = jnp.zeros_like(rise)
    rise[rise.shape[0] - ramp_rows :, :] = -ramp
    fetch.wait()
    heads[...] = lead[...].astype(BF16)
    total = None
    for q in range(GROUP - 1):
        found = matmul(heads[:, HOP * q : HOP * q + HOP], blocks[HOP * q : HOP * q + HOP, :])
        total = found if total is None else total + found
        sums[q] = total


def tables(taps, record):
    channels = record.shape[0]
    lead = L - HOP + JITTER
    vmem = pl.BlockSpec(memory_space=pltpu.VMEM)
    return pl.pallas_call(
        tables_kernel,
        out_shape=(
            jax.ShapeDtypeStruct((L, LANES), BF16),
            jax.ShapeDtypeStruct((EDGE, LANES), F32),
            jax.ShapeDtypeStruct((2 * JITTER, LANES), F32),
            jax.ShapeDtypeStruct((channels, lead), BF16),
            jax.ShapeDtypeStruct((GROUP - 1, channels, LANES), F32),
        ),
        in_specs=[vmem, pl.BlockSpec(memory_space=pl.ANY)],
        out_specs=(vmem,) * 5,
        scratch_shapes=[
            pltpu.VMEM((2 * TAPS + 6, LANES), F32),
            pltpu.VMEM((channels, lead), F32),
            pltpu.SemaphoreType.DMA,
        ],
        compiler_params=pltpu.CompilerParams(vmem_limit_bytes=50 * MIB),
        name="tables",
    )(taps, record)


def border_kernel(inbox, heads, sums, rise, fall, parts, done, collected):
    channels = heads.shape[0]
    done[...] = jnp.zeros_like(done)
    head = inbox[0:16, :].astype(F32)[:1]
    lane = lax.broadcasted_iota(jnp.int32, (1, LANES), 1)

    def told(at):
        return jnp.sum(jnp.where(lane == at, head, 0.0)).astype(jnp.int32)

    for q in range(GROUP):
        offset = told(q)
        edges = edge_table(rise, fall, offset)
        if q == 0:
            part = matmul(heads[:, 0:JITTER], edges[RIM:])
        else:
            part = matmul(heads[:, HOP * q - RIM : HOP * q + JITTER], edges)
            part = part + turn(sums[q - 1], HOP * q + offset - (TAPS - 1))
        upright = across(part * told(GROUP + q).astype(F32))
        for c in range(collected.shape[0]):
            piece = upright[:, 128 * c : 128 * c + 128]
            collected[c, pl.ds(q, BINS, stride=2 * GROUP), :] = piece[:BINS]
            collected[c, pl.ds(GROUP + q, BINS, stride=2 * GROUP), :] = piece[BINS:]
    width = min(128, channels)
    for c in range(collected.shape[0]):
        block = collected[c, : 2 * GROUP * BINS].reshape(BINS, 2 * GROUP, 128).astype(BF16)
        parts[:, :, width * c : width * c + width] = block[:, :, :width]


def border_parts(inbox, heads, sums, rise, fall):
    channels = heads.shape[0]
    vmem = pl.BlockSpec(memory_space=pltpu.VMEM)
    return pl.pallas_call(
        border_kernel,
        out_shape=(jax.ShapeDtypeStruct((BINS, 2 * GROUP, channels), BF16), jax.ShapeDtypeStruct((8, 128), F32)),
        in_specs=[vmem] * 5,
        out_specs=(vmem, vmem),
        scratch_shapes=[pltpu.VMEM((max(channels // 128, 1), 2 * GROUP * BINS + 2 * GROUP, 128), F32)],
        compiler_params=pltpu.CompilerParams(vmem_limit_bytes=50 * MIB),
        cost_estimate=pl.CostEstimate(
            flops=2 * channels * LANES * 1536, bytes_accessed=8 * channels * L, transcendentals=0
        ),
        name="border_parts",
    )(inbox, heads, sums, rise, fall)


def spectra_kernel(offsets, valid, record, rim, blocks, rise, fall, order, out, samples, later, collected, sems):
    channels, slab = record.shape
    steps = slab // L
    windows = GROUP * steps

    def fetch(s):
        return pltpu.make_async_copy(
            record.at[:, pl.ds(L * s, L)], samples.at[:, pl.ds(RIM + L * s, L)], sems.at[s]
        )

    for s in range(steps):
        fetch(s).start()
    samples[:, 0:RIM] = rim[...].astype(F32)
    samples[:, RIM + slab :] = jnp.zeros((channels, samples.shape[1] - RIM - slab), F32)

    def block_sums(s):
        found = []
        for i in range(GROUP):
            begin = pl.multiple_of(RIM + L * s + HOP * i, 128)
            found.append(
                matmul(samples[:, pl.ds(begin, HOP)].astype(BF16), blocks[HOP * i : HOP * i + HOP, :])
            )
        return found

    def keep(found):
        total = found[GROUP - 1]
        later[GROUP - 1] = total
        for q in range(GROUP - 2, -1, -1):
            total = total + found[q]
            later[q] = total

    def one_window(w, q, before):
        offset = offsets[w]
        begin = pl.multiple_of(HOP * w, 128)
        ends = samples[:, pl.ds(begin + L, EDGE)] - samples[:, pl.ds(begin, EDGE)]
        part = matmul(ends.astype(BF16), edge_table(rise, fall, offset))
        total = later[q] if before is None else later[q] + before
        part = (part + turn(total, HOP * q + offset - (TAPS - 1))) * valid[w].astype(F32)
        upright = across(part)
        for c in range(collected.shape[0]):
            collected[c, pl.ds(w, LANES, stride=windows), :] = upright[:, 128 * c : 128 * c + 128]

    fetch(0).wait()
    keep(block_sums(0))

    @pl.loop(0, steps - 1)
    def _(s):
        fetch(s + 1).wait()
        found = block_sums(s + 1)
        before = None
        for q in range(GROUP):
            one_window(GROUP * s + q, q, before)
            before = found[q] if before is None else before + found[q]
        keep(found)

    for q in range(GROUP):
        one_window(GROUP * (steps - 1) + q, q, None)

    width = min(128, channels)
    for c in range(collected.shape[0]):
        block = collected[c, : LANES * windows].reshape(LANES, windows, 128).astype(BF16)
        for ri in range(2):
            part = block[BINS * ri : BINS * ri + BINS, :, :width]
            out[:, windows * ri : windows * ri + windows, width * c : width * c + width] = part


def own_spectra(record, rim, offsets, valid, transform, rise, fall, order):
    channels, slab = record.shape
    windows = offsets.shape[0]
    smem = pl.BlockSpec(memory_space=pltpu.SMEM)
    vmem = pl.BlockSpec(memory_space=pltpu.VMEM)
    return pl.pallas_call(
        spectra_kernel,
        out_shape=jax.ShapeDtypeStruct((BINS, 2 * windows, channels), BF16),
        in_specs=[smem, smem, pl.BlockSpec(memory_space=pl.ANY), vmem, vmem, vmem, vmem, vmem],
        out_specs=vmem,
        scratch_shapes=[
            pltpu.VMEM((channels, RIM + slab + L - HOP + JITTER), F32),
            pltpu.VMEM((GROUP, channels, LANES), F32),
            pltpu.VMEM((max(channels // 128, 1), LANES * windows + windows, 128), F32),
            pltpu.SemaphoreType.DMA((slab // L,)),
        ],
        compiler_params=pltpu.CompilerParams(vmem_limit_bytes=50 * MIB),
        cost_estimate=pl.CostEstimate(
            flops=2 * channels * LANES * 896 * windows, bytes_accessed=4 * channels * slab, transcendentals=0
        ),
        name="own_spectra",
    )(offsets, valid, record, rim, transform, rise, fall, order)


def with_parts(block, part):
    windows = block.shape[1] // 2
    row = lax.broadcasted_iota(jnp.int32, part.shape, 1)
    moved = jnp.concatenate([part[:, GROUP:], part[:, :GROUP]], axis=1)
    pieces = []
    for ri, extra in enumerate((moved, part)):
        end = windows * ri + windows
        pieces.append(block[:, windows * ri : end - 2 * GROUP])
        pieces.append(block[:, end - 2 * GROUP : end] + jnp.where(row >= GROUP, extra, 0.0))
    return jnp.concatenate(pieces, axis=1)


def join_kernel(skip, own, parts, *chunks):
    *chunks, done = chunks
    done[...] = jnp.zeros_like(done)
    devices = chunks[0].shape[0]
    total = sum(chunk.shape[1] for chunk in chunks)
    for group in range(devices):
        begin = group * BINS // devices + skip
        end = begin + total
        joined = with_parts(own[begin:end].astype(F32), parts[begin:end].astype(F32)).astype(BF16)
        at = 0
        for chunk in chunks:
            chunk[group] = joined[at : at + chunk.shape[1]]
            at += chunk.shape[1]


def chunk_sizes(bins):
    count = min(3, bins)
    return [(bins + count - 1 - c) // count for c in range(count)]


def joined_chunks(own, parts, devices, skip, sizes):
    _, rows, channels = own.shape
    vmem = pl.BlockSpec(memory_space=pltpu.VMEM)
    *chunks, done = pl.pallas_call(
        functools.partial(join_kernel, skip),
        out_shape=tuple(jax.ShapeDtypeStruct((devices, count, rows, channels), BF16) for count in sizes)
        + (jax.ShapeDtypeStruct((8, 128), F32),),
        in_specs=[vmem, vmem],
        out_specs=(vmem,) * (len(sizes) + 1),
        compiler_params=pltpu.CompilerParams(vmem_limit_bytes=16 * MIB),
        name="joined_chunks",
    )(own, parts)
    return chunks, done


def left_kernel(own, out):
    sources, _, rows, channels = own.shape
    depth = sources * rows
    half = rows // 2
    straight = own[:, 0].astype(F32)
    turned = jnp.concatenate([straight[:, half:], -straight[:, :half]], axis=1)
    out[0, :channels] = straight.reshape(depth, channels).T.astype(BF16)
    out[0, channels:] = turned.reshape(depth, channels).T.astype(BF16)


def left_sides(own):
    sources, count, rows, channels = own.shape
    shape = (count, 2 * channels, sources * rows)
    return pl.pallas_call(
        left_kernel,
        grid=(count,),
        out_shape=jax.ShapeDtypeStruct(shape, BF16),
        in_specs=[pl.BlockSpec((sources, 1, rows, channels), lambda f: (0, f, 0, 0))],
        out_specs=pl.BlockSpec((1,) + shape[1:], lambda f: (f, 0, 0)),
        compiler_params=pltpu.CompilerParams(vmem_limit_bytes=16 * MIB),
        name="left_sides",
    )(own)


def cross_kernel(scale, stacked, me, left, *rest):
    out, done = rest[-2:]
    done[...] = jnp.zeros_like(done)
    sources, _, rows, channels = rest[0].shape[-4:]
    blocks = out.shape[3] // channels
    tile = min(256, channels)
    for n in range(blocks):
        if stacked:
            right, at = rest[0][n], channels * n
        else:
            right, at = rest[n][...], pl.multiple_of(channels * ((me[0] ^ n) & (blocks - 1)), 128)
        right = right[:, 0].reshape(sources * rows, channels)
        for j in range(0, channels, tile):
            for ri in range(2):
                both = matmul(left[0, channels * ri : channels * ri + channels, :], right[:, j : j + tile]) * scale
                out[0, ri, :, pl.ds(at + j, tile)] = both.astype(BF16)


def cross_products(left, right, result, begin, bins, blocks, first):
    sources, count, rows, channels = (right if first is None else right[0]).shape[-4:]
    columns = blocks if first is None else len(right)
    shape = (bins, 2, channels, blocks * channels)
    operands = [lax.axis_index("chan").astype(jnp.int32).reshape(1), left]
    in_specs = [pl.BlockSpec((1,) + left.shape[1:], lambda f, me: (f, 0, 0))]
    if first is None:
        operands.append(right)
        in_specs.append(pl.BlockSpec((blocks, sources, 1, rows, channels), lambda f, me: (0, 0, f, 0, 0)))
    else:
        operands += right
        in_specs += [pl.BlockSpec((sources, 1, rows, channels), lambda f, me: (0, f, 0, 0))] * columns
    if result is None:
        result, aliases = operands[1], {}
    else:
        aliases = {len(operands): 0}
    operands.append(result)
    in_specs.append(pl.BlockSpec(memory_space=pl.ANY))

    def place(f, me):
        return begin + f, 0, 0, 0 if first is None else (me[0] // columns) ^ (first // columns)

    return pl.pallas_call(
        functools.partial(cross_kernel, 2.0 / (sources * rows), first is None),
        grid_spec=pltpu.PrefetchScalarGridSpec(
            num_scalar_prefetch=1,
            grid=(count,),
            in_specs=in_specs,
            out_specs=(
                pl.BlockSpec((1, 2, channels, columns * channels), place),
                pl.BlockSpec((8, 128), lambda f, me: (0, 0)),
            ),
        ),
        out_shape=(jax.ShapeDtypeStruct(shape, BF16), jax.ShapeDtypeStruct((8, 128), F32)),
        input_output_aliases=aliases,
        compiler_params=pltpu.CompilerParams(vmem_limit_bytes=24 * MIB),
        cost_estimate=pl.CostEstimate(
            flops=4 * count * channels * columns * channels * sources * rows,
            bytes_accessed=4 * count * channels * columns * channels,
            transcendentals=0,
        ),
        name="cross_products",
    )(*operands)


def swapped(shard, axis, bit):
    devices = lax.axis_size(axis)
    return lax.ppermute(shard, axis, [(i, i ^ bit) for i in range(devices)])


def fan(shard, axis, bit):
    held = {0: shard}
    while bit:
        held.update({n | bit: swapped(block, axis, bit) for n, block in list(held.items())})
        bit //= 2
    return held


def after_kernel(shard, done, out):
    out[...] = shard[...]


def after(shard, done):
    if done is None:
        return shard
    vmem = pl.BlockSpec(memory_space=pltpu.VMEM)
    return pl.pallas_call(
        after_kernel,
        out_shape=jax.ShapeDtypeStruct(shard.shape, shard.dtype),
        in_specs=[vmem, vmem],
        out_specs=vmem,
        compiler_params=pltpu.CompilerParams(vmem_limit_bytes=8 * MIB),
        name="after",
    )(shard, done)


def per_device(record, whitening, offsets, window_valid):
    devices = lax.axis_size("tm")
    blocks = lax.axis_size("chan")
    stacked = blocks & (blocks - 1) != 0 or record.shape[0] % 128 != 0
    top = blocks // 2
    bins = BINS // devices

    def exchanged(chunk):
        return lax.all_to_all(chunk, "tm", split_axis=0, concat_axis=0, tiled=True)

    def fanned(shard):
        held = fan(shard, "chan", top // 2)
        return [held[n] for n in range(top)]

    inbox, taps = outbox(record, offsets, window_valid, whitening)
    inbox = from_behind(inbox, "tm", 1)
    transform, rise, fall, heads, sums = tables(taps, record)
    parts, done = border_parts(inbox, heads, sums, rise, fall)
    parts = from_behind(parts, "tm", -1)
    own = own_spectra(record, inbox, offsets, window_valid, transform, rise, fall, done)
    sizes = chunk_sizes(bins)
    begins = [sum(sizes[:p]) for p in range(len(sizes))]
    chunks, _ = joined_chunks(own, parts, devices, 0, sizes[:1])
    more, joined = joined_chunks(own, parts, devices, sizes[0], sizes[1:])
    chunks += more
    result, near, far, left, done = None, [], [], [], joined

    def cross(p, right, first):
        return cross_products(left[p], right, result, begins[p], bins, blocks, first)

    for p, chunk in enumerate(chunks):
        mine = exchanged(chunk)
        if stacked:
            right = lax.all_gather(mine, "chan", axis=0, tiled=False)
            result, _ = cross_products(left_sides(mine), right, result, begins[p], bins, blocks, None)
            continue
        mine = after(mine, done)
        far.append(swapped(mine, "chan", top))
        near.append(fanned(mine))
        left.append(left_sides(mine))
        ready = done
        result, done = cross(p, near[p], 0)
        if p:
            far[p - 1] = fanned(after(far[p - 1], ready) if p > 1 else far[p - 1])
            result, done = cross(p - 1, far[p - 1], top)
    if not stacked:
        for n, block in enumerate(fanned(after(far[-1], done))):
            result, _ = cross(len(chunks) - 1, [block], top + n)
    return result


def solution(mesh):
    in_specs = (P("chan", "tm"), P(), P("tm"), P("tm"))
    out_specs = P("tm", None, "chan", None)
    return jax.shard_map(
        per_device, mesh=mesh, in_specs=in_specs, out_specs=out_specs, check_vma=False
    )
```

profile of v0, /device:TPU:0, one launch (start us, length us, event | category | flops | bytes accessed | tf_op | source)
XLA Modules:
  0.0 116.6 jit_solution(9446111777819413269)
XLA Ops:
  0.0 1.7 %outbox.1 = (bf16[512,128]{1,0:T(8,128)(2,1)}, f32[72,128]{1,0:T(8,128)}) custom-call(s32[16]{0:T(128)} %offsets.3, s32[16]{0:T(128)} %valid.3, f32[65]{0:T(128)} %whitening.1, f32[512,8192]{1,0:T(8,128)} %record.5), custom_call_target="tpu_custom_call" | custom-call | tf_op jit(solution)/shard_map/outbox/pallas_call | solution.py:78
  1.7 4.9 %collective-permute-start = (bf16[512,128]{1,0:T(8,128)(2,1)}, bf16[512,128]{1,0:T(8,128)(2,1)S(1)}, u32[]{:S(2)}, u32[]{:S(2)}) collective-permute-start(bf16[512,128]{1,0:T(8,128)(2,1)} %get-tuple-element.28), channel_id=1, source_target_pairs={{0,1},{1,2},{2,3},{3,4},{4,5},{5,6},{6,7},{8,9},{9,10},{10,11},{11... | collective-permute-start | bytes 393224 | tf_op jit(solution)/shard_map/ppermute | solution.py:29
  7.3 2.7 %tables.1 = (bf16[2048,128]{1,0:T(8,128)(2,1)S(1)}, f32[384,128]{1,0:T(8,128)S(1)}, f32[512,128]{1,0:T(8,128)S(1)}, bf16[512,1792]{1,0:T(8,128)(2,1)S(1)}, f32[3,512,128]{2,1,0:T(8,128)S(1)}) custom-call(f32[72,128]{1,0:T(8,128)S(1)} %copy-done.5, f32[512,8192]{1,0:T(8,128)} %record.5), custom_call_target="tpu_custom_call" | custom-call | tf_op jit(solution)/shard_map/tables/pallas_call | solution.py:146
  10.9 1.3 %collective-permute-start.1 = (bf16[64,8,512]{2,1,0:T(8,128)(2,1)S(1)}, bf16[64,8,512]{2,1,0:T(8,128)(2,1)S(1)}, u32[]{:S(2)}, u32[]{:S(2)}) collective-permute-start(bf16[64,8,512]{2,1,0:T(8,128)(2,1)S(1)} %get-tuple-element.36), channel_id=1, source_target_pairs={{1,0},{2,1},{3,2},{4,3},{5,4},{6,5},{7,6},{9,8},{10,9},{11,10},{12... | collective-permute-start | bytes 1572872 | tf_op jit(solution)/shard_map/ppermute | solution.py:29
  12.3 10.2 %own_spectra.1.own = bf16[64,32,512]{2,1,0:T(8,128)(2,1)S(1)} custom-call(s32[16]{0:T(128)S(1)} %copy-done.6, s32[16]{0:T(128)S(1)} %copy-done.7, f32[512,8192]{1,0:T(8,128)} %record.5, bf16[512,128]{1,0:T(8,128)(2,1)S(1)} %collective-permute-done.inbox.rim, bf16[2048,128]{1,0:T(8,128)(2,1)S(1)} %get-tuple-element.30.blocks, ...), custom_call_target="tpu_custom_call" | custom-call | flops 1879048192 | bytes 16777216 | tf_op jit(solution)/shard_map/own_spectra/pallas_call | solution.py:283
  22.5 3.7 %collective-permute-done.1.parts = bf16[64,8,512]{2,1,0:T(8,128)(2,1)S(1)} collective-permute-done((bf16[64,8,512]{2,1,0:T(8,128)(2,1)S(1)}, bf16[64,8,512]{2,1,0:T(8,128)(2,1)S(1)}, u32[]{:S(2)}, u32[]{:S(2)}) %collective-permute-start.1) | collective-permute-done | bytes 524320 | tf_op jit(solution)/shard_map/ppermute | solution.py:29
  27.7 5.7 %all-to-all-start.1 = ((bf16[8,3,32,512]{3,2,1,0:T(8,128)(2,1)}), bf16[8,3,32,512]{3,2,1,0:T(8,128)(2,1)S(1)}, u32[]{:S(2)}, u32[]{:S(2)}) async-start(bf16[8,3,32,512]{3,2,1,0:T(8,128)(2,1)} %copy-done.3), calls=%async_computation.1 | async-start | bytes 1572864 | tf_op jit(solution)/shard_map/all_to_all | solution.py:475
  35.3 16.7 %all-to-all-done.1.shard = bf16[8,3,32,512]{3,2,1,0:T(8,128)(2,1)S(1)} async-done(((bf16[8,3,32,512]{3,2,1,0:T(8,128)(2,1)}), bf16[8,3,32,512]{3,2,1,0:T(8,128)(2,1)S(1)}, u32[]{:S(2)}, u32[]{:S(2)}) %all-to-all-start.1) | async-done | bytes 786464 | tf_op jit(solution)/shard_map/all_to_all | solution.py:475
  52.1 3.5 %all-to-all-start.2 = ((bf16[8,3,32,512]{3,2,1,0:T(8,128)(2,1)}), bf16[8,3,32,512]{3,2,1,0:T(8,128)(2,1)S(1)}, u32[]{:S(2)}, u32[]{:S(2)}) async-start(bf16[8,3,32,512]{3,2,1,0:T(8,128)(2,1)} %copy-done.2), calls=%async_computation.2 | async-start | bytes 1572864 | tf_op jit(solution)/shard_map/all_to_all | solution.py:475
  55.8 1.6 %collective-permute-start.2 = (bf16[8,3,32,512]{3,2,1,0:T(8,128)(2,1)S(1)}, bf16[8,3,32,512]{3,2,1,0:T(8,128)(2,1)}, u32[]{:S(2)}, u32[]{:S(2)}) collective-permute-start(bf16[8,3,32,512]{3,2,1,0:T(8,128)(2,1)S(1)} %after.5.own.rest_0_), channel_id=1, source_target_pairs={{0,16},{8,24},{16,0},{24,8},{1,17},{9,25},{17,1},{25,9},{2,18},{10... | collective-permute-start | bytes 2359304 | tf_op jit(solution)/shard_map/ppermute | solution.py:438
  58.1 4.2 %cross_products.7 = (bf16[8,2,512,2048]{3,2,1,0:T(8,128)(2,1)}, f32[8,128]{1,0:T(8,128)S(1)}) custom-call(s32[1]{0:T(128)} %bitcast.me, bf16[3,1024,256]{2,1,0:T(8,128)(2,1)S(1)} %left_sides.3.left.rest_2_, bf16[8,3,32,512]{3,2,1,0:T(8,128)(2,1)S(1)} %after.5.own.rest_0_, bf16[8,3,32,512]{3,2,1,0:T(8,128)(2,1)S(1)} %collective-permute-done.4.rest_1_, ...), custom_call_target="tpu_custom_call" | custom-call | flops 1610612736 | bytes 6291456 | tf_op jit(solution)/shard_map/cross_products/pallas_call | solution.py:413
  62.2 1.2 %copy-done = bf16[3,1024,256]{2,1,0:T(8,128)(2,1)} copy-done((bf16[3,1024,256]{2,1,0:T(8,128)(2,1)}, bf16[3,1024,256]{2,1,0:T(8,128)(2,1)S(1)}, u32[]{:S(2)}) %copy-start) | copy-done | bytes 1572888
  63.4 11.8 %all-to-all-done.2.shard = bf16[8,3,32,512]{3,2,1,0:T(8,128)(2,1)S(1)} async-done(((bf16[8,3,32,512]{3,2,1,0:T(8,128)(2,1)}), bf16[8,3,32,512]{3,2,1,0:T(8,128)(2,1)S(1)}, u32[]{:S(2)}, u32[]{:S(2)}) %all-to-all-start.2) | async-done | bytes 786464 | tf_op jit(solution)/shard_map/all_to_all | solution.py:475
  75.8 1.5 %collective-permute-start.7 = (bf16[8,3,32,512]{3,2,1,0:T(8,128)(2,1)S(1)}, bf16[8,3,32,512]{3,2,1,0:T(8,128)(2,1)}, u32[]{:S(2)}, u32[]{:S(2)}) collective-permute-start(bf16[8,3,32,512]{3,2,1,0:T(8,128)(2,1)S(1)} %after.6.own.rest_0_), channel_id=1, source_target_pairs={{0,16},{8,24},{16,0},{24,8},{1,17},{9,25},{17,1},{25,9},{2,18},{10... | collective-permute-start | bytes 2359304 | tf_op jit(solution)/shard_map/ppermute | solution.py:438
  77.3 6.0 %all-to-all-start = ((bf16[8,2,32,512]{3,2,1,0:T(8,128)(2,1)}), bf16[8,2,32,512]{3,2,1,0:T(8,128)(2,1)S(1)}, u32[]{:S(2)}, u32[]{:S(2)}) async-start(bf16[8,2,32,512]{3,2,1,0:T(8,128)(2,1)} %copy-done.4), calls=%async_computation | async-start | bytes 1048576 | tf_op jit(solution)/shard_map/all_to_all | solution.py:475
  84.1 5.1 %cross_products.8 = (bf16[8,2,512,2048]{3,2,1,0:T(8,128)(2,1)}, f32[8,128]{1,0:T(8,128)}) custom-call(s32[1]{0:T(128)} %bitcast.me, bf16[3,1024,256]{2,1,0:T(8,128)(2,1)S(1)} %left_sides.4.left, bf16[8,3,32,512]{3,2,1,0:T(8,128)(2,1)S(1)} %after.6.own.rest_0_, ...), custom_call_target="tpu_custom_call", output_to_operand_aliasing={{0}: (4, {})} | custom-call | flops 1610612736 | bytes 6291456 | tf_op jit(solution)/shard_map/cross_products/pallas_call | solution.py:413
  89.1 5.2 %cross_products.9 = (bf16[8,2,512,2048]{3,2,1,0:T(8,128)(2,1)}, f32[8,128]{1,0:T(8,128)S(1)}) custom-call(s32[1]{0:T(128)} %bitcast.me, bf16[3,1024,256]{2,1,0:T(8,128)(2,1)S(1)} %copy-done.1, bf16[8,3,32,512]{3,2,1,0:T(8,128)(2,1)} %collective-permute-done.2.rest_0_, ...), custom_call_target="tpu_custom_call", output_to_operand_aliasing={{0}: (4, {})} | custom-call | flops 1610612736 | bytes 6291456 | tf_op jit(solution)/shard_map/cross_products/pallas_call | solution.py:413
  94.4 1.5 %collective-permute-done.7.shard = bf16[8,3,32,512]{3,2,1,0:T(8,128)(2,1)} collective-permute-done((bf16[8,3,32,512]{3,2,1,0:T(8,128)(2,1)S(1)}, bf16[8,3,32,512]{3,2,1,0:T(8,128)(2,1)}, u32[]{:S(2)}, u32[]{:S(2)}) %collective-permute-start.7) | collective-permute-done | bytes 786464 | tf_op jit(solution)/shard_map/ppermute | solution.py:438
  95.9 1.2 %after.8.rest_0_ = bf16[8,3,32,512]{3,2,1,0:T(8,128)(2,1)S(1)} custom-call(bf16[8,3,32,512]{3,2,1,0:T(8,128)(2,1)} %collective-permute-done.7.shard, f32[8,128]{1,0:T(8,128)S(1)} %get-tuple-element.44.done), custom_call_target="tpu_custom_call" | custom-call | tf_op jit(solution)/shard_map/after/pallas_call | solution.py:457
  100.2 2.9 %cross_products.10 = (bf16[8,2,512,2048]{3,2,1,0:T(8,128)(2,1)}, f32[8,128]{1,0:T(8,128)}) custom-call(s32[1]{0:T(128)} %bitcast.me, bf16[2,1024,256]{2,1,0:T(8,128)(2,1)S(1)} %left_sides.5.left, bf16[8,2,32,512]{3,2,1,0:T(8,128)(2,1)S(1)} %after.7.own.rest_0_, ...), custom_call_target="tpu_custom_call", output_to_operand_aliasing={{0}: (4, {})} | custom-call | flops 1073741824 | bytes 4194304 | tf_op jit(solution)/shard_map/cross_products/pallas_call | solution.py:413
  103.0 5.0 %cross_products.11 = (bf16[8,2,512,2048]{3,2,1,0:T(8,128)(2,1)}, f32[8,128]{1,0:T(8,128)S(1)}) custom-call(s32[1]{0:T(128)} %bitcast.me, bf16[3,1024,256]{2,1,0:T(8,128)(2,1)S(1)} %left_sides.4.left, bf16[8,3,32,512]{3,2,1,0:T(8,128)(2,1)S(1)} %after.8.rest_0_, ...), custom_call_target="tpu_custom_call", output_to_operand_aliasing={{0}: (4, {})} | custom-call | flops 1610612736 | bytes 6291456 | tf_op jit(solution)/shard_map/cross_products/pallas_call | solution.py:413
  108.1 4.5 %collective-permute-done.6.shard = bf16[8,2,32,512]{3,2,1,0:T(8,128)(2,1)S(1)} collective-permute-done((bf16[8,2,32,512]{3,2,1,0:T(8,128)(2,1)S(1)}, bf16[8,2,32,512]{3,2,1,0:T(8,128)(2,1)S(1)}, u32[]{:S(2)}, u32[]{:S(2)}) %collective-permute-start.6) | collective-permute-done | bytes 524320 | tf_op jit(solution)/shard_map/ppermute | solution.py:438
  112.7 1.9 %cross_products.12 = (bf16[8,2,512,2048]{3,2,1,0:T(8,128)(2,1)}, f32[8,128]{1,0:T(8,128)}) custom-call(s32[1]{0:T(128)} %bitcast.me, bf16[2,1024,256]{2,1,0:T(8,128)(2,1)S(1)} %left_sides.5.left, bf16[8,2,32,512]{3,2,1,0:T(8,128)(2,1)S(1)} %after.9.rest_0_, bf16[8,2,512,2048]{3,2,1,0:T(8,128)(2,1)} %get-tuple-element.48.rest_1_), custom_call_target="tpu_custom_call", output_to_operand_aliasing={{0}: (3, {})} | custom-call | flops 536870912 | bytes 2097152 | tf_op jit(solution)/shard_map/cross_products/pallas_call | solution.py:413
  114.7 1.9 %cross_products.13 = (bf16[8,2,512,2048]{3,2,1,0:T(8,128)(2,1)}, f32[8,128]{1,0:T(8,128)}) custom-call(s32[1]{0:T(128)} %bitcast.me, bf16[2,1024,256]{2,1,0:T(8,128)(2,1)S(1)} %left_sides.5.left, bf16[8,2,32,512]{3,2,1,0:T(8,128)(2,1)S(1)} %collective-permute-done.10.rest_0_, ...), custom_call_target="tpu_custom_call", output_to_operand_aliasing={{0}: (3, {})} | custom-call | flops 536870912 | bytes 2097152 | tf_op jit(solution)/shard_map/cross_products/pallas_call | solution.py:413
  (41 shorter events, 10.5 us)
Async XLA Ops:
  0.0 12.2 %copy-start.6 = (s32[16]{0:T(128)S(1)}, s32[16]{0:T(128)}, u32[]{:S(2)}) copy-start(s32[16]{0:T(128)} %offsets.3) | copy-start | bytes 196
  0.0 12.3 %copy-start.7 = (s32[16]{0:T(128)S(1)}, s32[16]{0:T(128)}, u32[]{:S(2)}) copy-start(s32[16]{0:T(128)} %valid.3) | copy-start | bytes 196
  1.7 8.4 %collective-permute-start = (bf16[512,128]{1,0:T(8,128)(2,1)}, bf16[512,128]{1,0:T(8,128)(2,1)S(1)}, u32[]{:S(2)}, u32[]{:S(2)}) collective-permute-start(bf16[512,128]{1,0:T(8,128)(2,1)} %get-tuple-element.28), channel_id=1, source_target_pairs={{0,1},{1,2},{2,3},{3,4},{4,5},{5,6},{6,7},{8,9},{9,10},{10,11},{11... | collective-permute-start | bytes 393224 | tf_op jit(solution)/shard_map/ppermute | solution.py:29
  6.6 0.8 copy-start.5
  10.9 15.2 %collective-permute-start.1 = (bf16[64,8,512]{2,1,0:T(8,128)(2,1)S(1)}, bf16[64,8,512]{2,1,0:T(8,128)(2,1)S(1)}, u32[]{:S(2)}, u32[]{:S(2)}) collective-permute-start(bf16[64,8,512]{2,1,0:T(8,128)(2,1)S(1)} %get-tuple-element.36), channel_id=1, source_target_pairs={{1,0},{2,1},{3,2},{4,3},{5,4},{6,5},{7,6},{9,8},{10,9},{11,10},{12... | collective-permute-start | bytes 1572872 | tf_op jit(solution)/shard_map/ppermute | solution.py:29
  26.8 0.9 copy-start.3
  27.7 24.4 %all-to-all-start.1 = ((bf16[8,3,32,512]{3,2,1,0:T(8,128)(2,1)}), bf16[8,3,32,512]{3,2,1,0:T(8,128)(2,1)S(1)}, u32[]{:S(2)}, u32[]{:S(2)}) async-start(bf16[8,3,32,512]{3,2,1,0:T(8,128)(2,1)} %copy-done.3), calls=%async_computation.1 | async-start | bytes 1572864 | tf_op jit(solution)/shard_map/all_to_all | solution.py:475
  33.6 0.9 copy-start.2
  34.5 0.8 copy-start.4
  52.1 23.1 %all-to-all-start.2 = ((bf16[8,3,32,512]{3,2,1,0:T(8,128)(2,1)}), bf16[8,3,32,512]{3,2,1,0:T(8,128)(2,1)S(1)}, u32[]{:S(2)}, u32[]{:S(2)}) async-start(bf16[8,3,32,512]{3,2,1,0:T(8,128)(2,1)} %copy-done.2), calls=%async_computation.2 | async-start | bytes 1572864 | tf_op jit(solution)/shard_map/all_to_all | solution.py:475
  55.7 2.4 %collective-permute-start.4 = (bf16[8,3,32,512]{3,2,1,0:T(8,128)(2,1)S(1)}, bf16[8,3,32,512]{3,2,1,0:T(8,128)(2,1)S(1)}, u32[]{:S(2)}, u32[]{:S(2)}) collective-permute-start(bf16[8,3,32,512]{3,2,1,0:T(8,128)(2,1)S(1)} %after.5.own.rest_0_), channel_id=1, source_target_pairs={{0,8},{8,0},{16,24},{24,16},{1,9},{9,1},{17,25},{25,17},{2,10},{10... | collective-permute-start | bytes 2359304 | tf_op jit(solution)/shard_map/ppermute | solution.py:438
  55.8 20.1 %collective-permute-start.2 = (bf16[8,3,32,512]{3,2,1,0:T(8,128)(2,1)S(1)}, bf16[8,3,32,512]{3,2,1,0:T(8,128)(2,1)}, u32[]{:S(2)}, u32[]{:S(2)}) collective-permute-start(bf16[8,3,32,512]{3,2,1,0:T(8,128)(2,1)S(1)} %after.5.own.rest_0_), channel_id=1, source_target_pairs={{0,16},{8,24},{16,0},{24,8},{1,17},{9,25},{17,1},{25,9},{2,18},{10... | collective-permute-start | bytes 2359304 | tf_op jit(solution)/shard_map/ppermute | solution.py:438
  62.2 1.2 %copy-start = (bf16[3,1024,256]{2,1,0:T(8,128)(2,1)}, bf16[3,1024,256]{2,1,0:T(8,128)(2,1)S(1)}, u32[]{:S(2)}) copy-start(bf16[3,1024,256]{2,1,0:T(8,128)(2,1)S(1)} %left_sides.3.left.rest_2_) | copy-start | bytes 4718596
  75.2 8.8 %collective-permute-start.5 = (bf16[8,3,32,512]{3,2,1,0:T(8,128)(2,1)S(1)}, bf16[8,3,32,512]{3,2,1,0:T(8,128)(2,1)}, u32[]{:S(2)}, u32[]{:S(2)}) collective-permute-start(bf16[8,3,32,512]{3,2,1,0:T(8,128)(2,1)S(1)} %after.6.own.rest_0_), channel_id=1, source_target_pairs={{0,8},{8,0},{16,24},{24,16},{1,9},{9,1},{17,25},{25,17},{2,10},{10... | collective-permute-start | bytes 2359304 | tf_op jit(solution)/shard_map/ppermute | solution.py:438
  75.8 13.3 %collective-permute-start.3 = (bf16[8,3,32,512]{3,2,1,0:T(8,128)(2,1)}, bf16[8,3,32,512]{3,2,1,0:T(8,128)(2,1)}, u32[]{:S(2)}, u32[]{:S(2)}) collective-permute-start(bf16[8,3,32,512]{3,2,1,0:T(8,128)(2,1)} %collective-permute-done.2.rest_0_), channel_id=1, source_target_pairs={{0,8},{8,0},{16,24},{24,16},{1,9},{9,1},{17,25},{25,17},{2,10},{10... | collective-permute-start | bytes 2359304 | tf_op jit(solution)/shard_map/ppermute | solution.py:438
  75.8 20.1 %collective-permute-start.7 = (bf16[8,3,32,512]{3,2,1,0:T(8,128)(2,1)S(1)}, bf16[8,3,32,512]{3,2,1,0:T(8,128)(2,1)}, u32[]{:S(2)}, u32[]{:S(2)}) collective-permute-start(bf16[8,3,32,512]{3,2,1,0:T(8,128)(2,1)S(1)} %after.6.own.rest_0_), channel_id=1, source_target_pairs={{0,16},{8,24},{16,0},{24,8},{1,17},{9,25},{17,1},{25,9},{2,18},{10... | collective-permute-start | bytes 2359304 | tf_op jit(solution)/shard_map/ppermute | solution.py:438
  77.3 20.9 %all-to-all-start = ((bf16[8,2,32,512]{3,2,1,0:T(8,128)(2,1)}), bf16[8,2,32,512]{3,2,1,0:T(8,128)(2,1)S(1)}, u32[]{:S(2)}, u32[]{:S(2)}) async-start(bf16[8,2,32,512]{3,2,1,0:T(8,128)(2,1)} %copy-done.4), calls=%async_computation | async-start | bytes 1048576 | tf_op jit(solution)/shard_map/all_to_all | solution.py:475
  83.3 5.8 %copy-start.1 = (bf16[3,1024,256]{2,1,0:T(8,128)(2,1)S(1)}, bf16[3,1024,256]{2,1,0:T(8,128)(2,1)}, u32[]{:S(2)}) copy-start(bf16[3,1024,256]{2,1,0:T(8,128)(2,1)} %copy-done) | copy-start | bytes 4718596
  97.1 6.0 %collective-permute-start.8 = (bf16[8,3,32,512]{3,2,1,0:T(8,128)(2,1)S(1)}, bf16[8,3,32,512]{3,2,1,0:T(8,128)(2,1)}, u32[]{:S(2)}, u32[]{:S(2)}) collective-permute-start(bf16[8,3,32,512]{3,2,1,0:T(8,128)(2,1)S(1)} %after.8.rest_0_), channel_id=1, source_target_pairs={{0,8},{8,0},{16,24},{24,16},{1,9},{9,1},{17,25},{25,17},{2,10},{10... | collective-permute-start | bytes 2359304 | tf_op jit(solution)/shard_map/ppermute | solution.py:438
  98.2 2.0 %collective-permute-start.9 = (bf16[8,2,32,512]{3,2,1,0:T(8,128)(2,1)S(1)}, bf16[8,2,32,512]{3,2,1,0:T(8,128)(2,1)S(1)}, u32[]{:S(2)}, u32[]{:S(2)}) collective-permute-start(bf16[8,2,32,512]{3,2,1,0:T(8,128)(2,1)S(1)} %after.7.own.rest_0_), channel_id=1, source_target_pairs={{0,8},{8,0},{16,24},{24,16},{1,9},{9,1},{17,25},{25,17},{2,10},{10... | collective-permute-start | bytes 1572872 | tf_op jit(solution)/shard_map/ppermute | solution.py:438
  98.3 14.3 %collective-permute-start.6 = (bf16[8,2,32,512]{3,2,1,0:T(8,128)(2,1)S(1)}, bf16[8,2,32,512]{3,2,1,0:T(8,128)(2,1)S(1)}, u32[]{:S(2)}, u32[]{:S(2)}) collective-permute-start(bf16[8,2,32,512]{3,2,1,0:T(8,128)(2,1)S(1)} %after.7.own.rest_0_), channel_id=1, source_target_pairs={{0,16},{8,24},{16,0},{24,8},{1,17},{9,25},{17,1},{25,9},{2,18},{10... | collective-permute-start | bytes 1572872 | tf_op jit(solution)/shard_map/ppermute | solution.py:438
  112.7 2.0 %collective-permute-start.10 = (bf16[8,2,32,512]{3,2,1,0:T(8,128)(2,1)S(1)}, bf16[8,2,32,512]{3,2,1,0:T(8,128)(2,1)S(1)}, u32[]{:S(2)}, u32[]{:S(2)}) collective-permute-start(bf16[8,2,32,512]{3,2,1,0:T(8,128)(2,1)S(1)} %after.9.rest_0_), channel_id=1, source_target_pairs={{0,8},{8,0},{16,24},{24,16},{1,9},{9,1},{17,25},{25,17},{2,10},{10... | collective-permute-start | bytes 1572872 | tf_op jit(solution)/shard_map/ppermute | solution.py:438
where the time goes:
time: 117 us
  Pallas kernels  45.9 us (39%)
  waiting for transfers between devices  40.2 us (34%)
  starting transfers between devices  25.8 us (22%)
  local copies, waits for them, and re-layouts  4.51 us (4%)
    all_to_all x3, waiting for transfers between devices, exchanged(): return lax.all_to_all(chunk, 'tm', split_axis=0, concat_axis=0, tiled=True)  29.5 us
    pallas_call x7, Pallas kernels, cross_products(): pl.pallas_call(functools.partial(cross_kernel, 2.0 / (sources * rows), fi...  26.2 us
    all_to_all x3, starting transfers between devices, exchanged(): return lax.all_to_all(chunk, 'tm', split_axis=0, concat_axis=0, tiled=True)  15.3 us
    pallas_call x1, Pallas kernels, own_spectra(): pl.pallas_call(spectra_kernel, out_shape=jax.ShapeDtypeStruct((BINS, 2 *...  10.2 us
    ppermute x9, waiting for transfers between devices, swapped(): return lax.ppermute(shard, axis, [(i, i ^ bit) for i in range(devices)])  7.03 us
    ppermute x2, starting transfers between devices, from_behind(): return lax.ppermute(shard, axis, pairs)  6.16 us
    unnamed x16, local copies, waits for them, and re-layouts  4.51 us
    ppermute x9, starting transfers between devices, swapped(): return lax.ppermute(shard, axis, [(i, i ^ bit) for i in range(devices)])  4.36 us
  transfers between devices with their start and end apart: 14, of which 8 were waited for; matrix products, arithmetic and copies ran while one was open for 0% of the time, Pallas kernels for 35%

commit v1 on v0

--- a/solution.py
+++ b/solution.py
@@ -383,9 +383,9 @@
             right, at = rest[n][...], pl.multiple_of(channels * ((me[0] ^ n) & (blocks - 1)), 128)
         right = right[:, 0].reshape(sources * rows, channels)
         for j in range(0, channels, tile):
-            for ri in range(2):
-                both = matmul(left[0, channels * ri : channels * ri + channels, :], right[:, j : j + tile]) * scale
-                out[0, ri, :, pl.ds(at + j, tile)] = both.astype(BF16)
+            for r in range(0, 2 * channels, tile):
+                both = matmul(left[0, r : r + tile, :], right[:, j : j + tile]) * scale
+                out[0, r // channels, r % channels : r % channels + tile, pl.ds(at + j, tile)] = both.astype(BF16)
 
 
 def cross_products(left, right, result, begin, bins, blocks, first):

time: 117 us -> 117 us (level)
  no operation moved by 1% of the time
where the time goes in v1:
time: 117 us
  Pallas kernels  45.9 us (39%)
  waiting for transfers between devices  40.3 us (34%)
  starting transfers between devices  25.7 us (22%)
  local copies, waits for them, and re-layouts  4.51 us (4%)
    all_to_all x3, waiting for transfers between devices, exchanged(): return lax.all_to_all(chunk, 'tm', split_axis=0, concat_axis=0, tiled=True)  29.5 us
    pallas_call x7, Pallas kernels, cross_products(): pl.pallas_call(functools.partial(cross_kernel, 2.0 / (sources * rows), fi...  26.2 us
    all_to_all x3, starting transfers between devices, exchanged(): return lax.all_to_all(chunk, 'tm', split_axis=0, concat_axis=0, tiled=True)  15.3 us
    pallas_call x1, Pallas kernels, own_spectra(): pl.pallas_call(spectra_kernel, out_shape=jax.ShapeDtypeStruct((BINS, 2 *...  10.2 us
    ppermute x9, waiting for transfers between devices, swapped(): return lax.ppermute(shard, axis, [(i, i ^ bit) for i in range(devices)])  7.06 us
    ppermute x2, starting transfers between devices, from_behind(): return lax.ppermute(shard, axis, pairs)  6.16 us
    unnamed x16, local copies, waits for them, and re-layouts  4.51 us
    ppermute x9, starting transfers between devices, swapped(): return lax.ppermute(shard, axis, [(i, i ^ bit) for i in range(devices)])  4.31 us
  transfers between devices with their start and end apart: 14, of which 8 were waited for; matrix products, arithmetic and copies ran while one was open for 0% of the time, Pallas kernels for 35%

profile of v1, /device:TPU:0, one launch (start us, length us, event | category | flops | bytes accessed | tf_op | source)
XLA Modules:
  0.0 116.6 jit_solution(1672979558826573377)
XLA Ops:
  0.0 1.7 %outbox.1 = (bf16[512,128]{1,0:T(8,128)(2,1)}, f32[72,128]{1,0:T(8,128)}) custom-call(s32[16]{0:T(128)} %offsets.3, s32[16]{0:T(128)} %valid.3, f32[65]{0:T(128)} %whitening.1, f32[512,8192]{1,0:T(8,128)} %record.5), custom_call_target="tpu_custom_call" | custom-call | tf_op jit(solution)/shard_map/outbox/pallas_call | solution.py:78
  1.7 4.9 %collective-permute-start = (bf16[512,128]{1,0:T(8,128)(2,1)}, bf16[512,128]{1,0:T(8,128)(2,1)S(1)}, u32[]{:S(2)}, u32[]{:S(2)}) collective-permute-start(bf16[512,128]{1,0:T(8,128)(2,1)} %get-tuple-element.28), channel_id=1, source_target_pairs={{0,1},{1,2},{2,3},{3,4},{4,5},{5,6},{6,7},{8,9},{9,10},{10,11},{11... | collective-permute-start | bytes 393224 | tf_op jit(solution)/shard_map/ppermute | solution.py:29
  7.3 2.7 %tables.1 = (bf16[2048,128]{1,0:T(8,128)(2,1)S(1)}, f32[384,128]{1,0:T(8,128)S(1)}, f32[512,128]{1,0:T(8,128)S(1)}, bf16[512,1792]{1,0:T(8,128)(2,1)S(1)}, f32[3,512,128]{2,1,0:T(8,128)S(1)}) custom-call(f32[72,128]{1,0:T(8,128)S(1)} %copy-done.5, f32[512,8192]{1,0:T(8,128)} %record.5), custom_call_target="tpu_custom_call" | custom-call | tf_op jit(solution)/shard_map/tables/pallas_call | solution.py:146
  10.9 1.3 %collective-permute-start.1 = (bf16[64,8,512]{2,1,0:T(8,128)(2,1)S(1)}, bf16[64,8,512]{2,1,0:T(8,128)(2,1)S(1)}, u32[]{:S(2)}, u32[]{:S(2)}) collective-permute-start(bf16[64,8,512]{2,1,0:T(8,128)(2,1)S(1)} %get-tuple-element.36), channel_id=1, source_target_pairs={{1,0},{2,1},{3,2},{4,3},{5,4},{6,5},{7,6},{9,8},{10,9},{11,10},{12... | collective-permute-start | bytes 1572872 | tf_op jit(solution)/shard_map/ppermute | solution.py:29
  12.2 10.2 %own_spectra.1.own = bf16[64,32,512]{2,1,0:T(8,128)(2,1)S(1)} custom-call(s32[16]{0:T(128)S(1)} %copy-done.6, s32[16]{0:T(128)S(1)} %copy-done.7, f32[512,8192]{1,0:T(8,128)} %record.5, bf16[512,128]{1,0:T(8,128)(2,1)S(1)} %collective-permute-done.inbox.rim, bf16[2048,128]{1,0:T(8,128)(2,1)S(1)} %get-tuple-element.30.blocks, ...), custom_call_target="tpu_custom_call" | custom-call | flops 1879048192 | bytes 16777216 | tf_op jit(solution)/shard_map/own_spectra/pallas_call | solution.py:283
  22.5 3.7 %collective-permute-done.1.parts = bf16[64,8,512]{2,1,0:T(8,128)(2,1)S(1)} collective-permute-done((bf16[64,8,512]{2,1,0:T(8,128)(2,1)S(1)}, bf16[64,8,512]{2,1,0:T(8,128)(2,1)S(1)}, u32[]{:S(2)}, u32[]{:S(2)}) %collective-permute-start.1) | collective-permute-done | bytes 524320 | tf_op jit(solution)/shard_map/ppermute | solution.py:29
  27.7 5.7 %all-to-all-start.1 = ((bf16[8,3,32,512]{3,2,1,0:T(8,128)(2,1)}), bf16[8,3,32,512]{3,2,1,0:T(8,128)(2,1)S(1)}, u32[]{:S(2)}, u32[]{:S(2)}) async-start(bf16[8,3,32,512]{3,2,1,0:T(8,128)(2,1)} %copy-done.3), calls=%async_computation.1 | async-start | bytes 1572864 | tf_op jit(solution)/shard_map/all_to_all | solution.py:475
  35.3 16.7 %all-to-all-done.1.shard = bf16[8,3,32,512]{3,2,1,0:T(8,128)(2,1)S(1)} async-done(((bf16[8,3,32,512]{3,2,1,0:T(8,128)(2,1)}), bf16[8,3,32,512]{3,2,1,0:T(8,128)(2,1)S(1)}, u32[]{:S(2)}, u32[]{:S(2)}) %all-to-all-start.1) | async-done | bytes 786464 | tf_op jit(solution)/shard_map/all_to_all | solution.py:475
  52.1 3.5 %all-to-all-start.2 = ((bf16[8,3,32,512]{3,2,1,0:T(8,128)(2,1)}), bf16[8,3,32,512]{3,2,1,0:T(8,128)(2,1)S(1)}, u32[]{:S(2)}, u32[]{:S(2)}) async-start(bf16[8,3,32,512]{3,2,1,0:T(8,128)(2,1)} %copy-done.2), calls=%async_computation.2 | async-start | bytes 1572864 | tf_op jit(solution)/shard_map/all_to_all | solution.py:475
  55.8 1.5 %collective-permute-start.2 = (bf16[8,3,32,512]{3,2,1,0:T(8,128)(2,1)S(1)}, bf16[8,3,32,512]{3,2,1,0:T(8,128)(2,1)}, u32[]{:S(2)}, u32[]{:S(2)}) collective-permute-start(bf16[8,3,32,512]{3,2,1,0:T(8,128)(2,1)S(1)} %after.5.own.rest_0_), channel_id=1, source_target_pairs={{0,16},{8,24},{16,0},{24,8},{1,17},{9,25},{17,1},{25,9},{2,18},{10... | collective-permute-start | bytes 2359304 | tf_op jit(solution)/shard_map/ppermute | solution.py:438
  58.0 4.2 %cross_products.7 = (bf16[8,2,512,2048]{3,2,1,0:T(8,128)(2,1)}, f32[8,128]{1,0:T(8,128)S(1)}) custom-call(s32[1]{0:T(128)} %bitcast.me, bf16[3,1024,256]{2,1,0:T(8,128)(2,1)S(1)} %left_sides.3.left.rest_2_, bf16[8,3,32,512]{3,2,1,0:T(8,128)(2,1)S(1)} %after.5.own.rest_0_, bf16[8,3,32,512]{3,2,1,0:T(8,128)(2,1)S(1)} %collective-permute-done.4.rest_1_, ...), custom_call_target="tpu_custom_call" | custom-call | flops 1610612736 | bytes 6291456 | tf_op jit(solution)/shard_map/cross_products/pallas_call | solution.py:413
  62.2 1.2 %copy-done = bf16[3,1024,256]{2,1,0:T(8,128)(2,1)} copy-done((bf16[3,1024,256]{2,1,0:T(8,128)(2,1)}, bf16[3,1024,256]{2,1,0:T(8,128)(2,1)S(1)}, u32[]{:S(2)}) %copy-start) | copy-done | bytes 1572888
  63.4 11.8 %all-to-all-done.2.shard = bf16[8,3,32,512]{3,2,1,0:T(8,128)(2,1)S(1)} async-done(((bf16[8,3,32,512]{3,2,1,0:T(8,128)(2,1)}), bf16[8,3,32,512]{3,2,1,0:T(8,128)(2,1)S(1)}, u32[]{:S(2)}, u32[]{:S(2)}) %all-to-all-start.2) | async-done | bytes 786464 | tf_op jit(solution)/shard_map/all_to_all | solution.py:475
  75.8 1.5 %collective-permute-start.7 = (bf16[8,3,32,512]{3,2,1,0:T(8,128)(2,1)S(1)}, bf16[8,3,32,512]{3,2,1,0:T(8,128)(2,1)}, u32[]{:S(2)}, u32[]{:S(2)}) collective-permute-start(bf16[8,3,32,512]{3,2,1,0:T(8,128)(2,1)S(1)} %after.6.own.rest_0_), channel_id=1, source_target_pairs={{0,16},{8,24},{16,0},{24,8},{1,17},{9,25},{17,1},{25,9},{2,18},{10... | collective-permute-start | bytes 2359304 | tf_op jit(solution)/shard_map/ppermute | solution.py:438
  77.3 6.0 %all-to-all-start = ((bf16[8,2,32,512]{3,2,1,0:T(8,128)(2,1)}), bf16[8,2,32,512]{3,2,1,0:T(8,128)(2,1)S(1)}, u32[]{:S(2)}, u32[]{:S(2)}) async-start(bf16[8,2,32,512]{3,2,1,0:T(8,128)(2,1)} %copy-done.4), calls=%async_computation | async-start | bytes 1048576 | tf_op jit(solution)/shard_map/all_to_all | solution.py:475
  84.0 5.1 %cross_products.8 = (bf16[8,2,512,2048]{3,2,1,0:T(8,128)(2,1)}, f32[8,128]{1,0:T(8,128)}) custom-call(s32[1]{0:T(128)} %bitcast.me, bf16[3,1024,256]{2,1,0:T(8,128)(2,1)S(1)} %left_sides.4.left, bf16[8,3,32,512]{3,2,1,0:T(8,128)(2,1)S(1)} %after.6.own.rest_0_, ...), custom_call_target="tpu_custom_call", output_to_operand_aliasing={{0}: (4, {})} | custom-call | flops 1610612736 | bytes 6291456 | tf_op jit(solution)/shard_map/cross_products/pallas_call | solution.py:413
  89.1 5.2 %cross_products.9 = (bf16[8,2,512,2048]{3,2,1,0:T(8,128)(2,1)}, f32[8,128]{1,0:T(8,128)S(1)}) custom-call(s32[1]{0:T(128)} %bitcast.me, bf16[3,1024,256]{2,1,0:T(8,128)(2,1)S(1)} %copy-done.1, bf16[8,3,32,512]{3,2,1,0:T(8,128)(2,1)} %collective-permute-done.2.rest_0_, ...), custom_call_target="tpu_custom_call", output_to_operand_aliasing={{0}: (4, {})} | custom-call | flops 1610612736 | bytes 6291456 | tf_op jit(solution)/shard_map/cross_products/pallas_call | solution.py:413
  94.3 1.5 %collective-permute-done.7.shard = bf16[8,3,32,512]{3,2,1,0:T(8,128)(2,1)} collective-permute-done((bf16[8,3,32,512]{3,2,1,0:T(8,128)(2,1)S(1)}, bf16[8,3,32,512]{3,2,1,0:T(8,128)(2,1)}, u32[]{:S(2)}, u32[]{:S(2)}) %collective-permute-start.7) | collective-permute-done | bytes 786464 | tf_op jit(solution)/shard_map/ppermute | solution.py:438
  95.9 1.2 %after.8.rest_0_ = bf16[8,3,32,512]{3,2,1,0:T(8,128)(2,1)S(1)} custom-call(bf16[8,3,32,512]{3,2,1,0:T(8,128)(2,1)} %collective-permute-done.7.shard, f32[8,128]{1,0:T(8,128)S(1)} %get-tuple-element.44.done), custom_call_target="tpu_custom_call" | custom-call | tf_op jit(solution)/shard_map/after/pallas_call | solution.py:457
  100.2 2.9 %cross_products.10 = (bf16[8,2,512,2048]{3,2,1,0:T(8,128)(2,1)}, f32[8,128]{1,0:T(8,128)}) custom-call(s32[1]{0:T(128)} %bitcast.me, bf16[2,1024,256]{2,1,0:T(8,128)(2,1)S(1)} %left_sides.5.left, bf16[8,2,32,512]{3,2,1,0:T(8,128)(2,1)S(1)} %after.7.own.rest_0_, ...), custom_call_target="tpu_custom_call", output_to_operand_aliasing={{0}: (4, {})} | custom-call | flops 1073741824 | bytes 4194304 | tf_op jit(solution)/shard_map/cross_products/pallas_call | solution.py:413
  103.0 5.0 %cross_products.11 = (bf16[8,2,512,2048]{3,2,1,0:T(8,128)(2,1)}, f32[8,128]{1,0:T(8,128)S(1)}) custom-call(s32[1]{0:T(128)} %bitcast.me, bf16[3,1024,256]{2,1,0:T(8,128)(2,1)S(1)} %left_sides.4.left, bf16[8,3,32,512]{3,2,1,0:T(8,128)(2,1)S(1)} %after.8.rest_0_, ...), custom_call_target="tpu_custom_call", output_to_operand_aliasing={{0}: (4, {})} | custom-call | flops 1610612736 | bytes 6291456 | tf_op jit(solution)/shard_map/cross_products/pallas_call | solution.py:413
  108.1 4.5 %collective-permute-done.6.shard = bf16[8,2,32,512]{3,2,1,0:T(8,128)(2,1)S(1)} collective-permute-done((bf16[8,2,32,512]{3,2,1,0:T(8,128)(2,1)S(1)}, bf16[8,2,32,512]{3,2,1,0:T(8,128)(2,1)S(1)}, u32[]{:S(2)}, u32[]{:S(2)}) %collective-permute-start.6) | collective-permute-done | bytes 524320 | tf_op jit(solution)/shard_map/ppermute | solution.py:438
  112.7 1.9 %cross_products.12 = (bf16[8,2,512,2048]{3,2,1,0:T(8,128)(2,1)}, f32[8,128]{1,0:T(8,128)}) custom-call(s32[1]{0:T(128)} %bitcast.me, bf16[2,1024,256]{2,1,0:T(8,128)(2,1)S(1)} %left_sides.5.left, bf16[8,2,32,512]{3,2,1,0:T(8,128)(2,1)S(1)} %after.9.rest_0_, bf16[8,2,512,2048]{3,2,1,0:T(8,128)(2,1)} %get-tuple-element.48.rest_1_), custom_call_target="tpu_custom_call", output_to_operand_aliasing={{0}: (3, {})} | custom-call | flops 536870912 | bytes 2097152 | tf_op jit(solution)/shard_map/cross_products/pallas_call | solution.py:413
  114.7 1.9 %cross_products.13 = (bf16[8,2,512,2048]{3,2,1,0:T(8,128)(2,1)}, f32[8,128]{1,0:T(8,128)}) custom-call(s32[1]{0:T(128)} %bitcast.me, bf16[2,1024,256]{2,1,0:T(8,128)(2,1)S(1)} %left_sides.5.left, bf16[8,2,32,512]{3,2,1,0:T(8,128)(2,1)S(1)} %collective-permute-done.10.rest_0_, ...), custom_call_target="tpu_custom_call", output_to_operand_aliasing={{0}: (3, {})} | custom-call | flops 536870912 | bytes 2097152 | tf_op jit(solution)/shard_map/cross_products/pallas_call | solution.py:413
  (41 shorter events, 10.5 us)
Async XLA Ops:
  0.0 12.2 %copy-start.6 = (s32[16]{0:T(128)S(1)}, s32[16]{0:T(128)}, u32[]{:S(2)}) copy-start(s32[16]{0:T(128)} %offsets.3) | copy-start | bytes 196
  0.0 12.2 %copy-start.7 = (s32[16]{0:T(128)S(1)}, s32[16]{0:T(128)}, u32[]{:S(2)}) copy-start(s32[16]{0:T(128)} %valid.3) | copy-start | bytes 196
  1.7 8.3 %collective-permute-start = (bf16[512,128]{1,0:T(8,128)(2,1)}, bf16[512,128]{1,0:T(8,128)(2,1)S(1)}, u32[]{:S(2)}, u32[]{:S(2)}) collective-permute-start(bf16[512,128]{1,0:T(8,128)(2,1)} %get-tuple-element.28), channel_id=1, source_target_pairs={{0,1},{1,2},{2,3},{3,4},{4,5},{5,6},{6,7},{8,9},{9,10},{10,11},{11... | collective-permute-start | bytes 393224 | tf_op jit(solution)/shard_map/ppermute | solution.py:29
  6.6 0.8 copy-start.5
  10.9 15.3 %collective-permute-start.1 = (bf16[64,8,512]{2,1,0:T(8,128)(2,1)S(1)}, bf16[64,8,512]{2,1,0:T(8,128)(2,1)S(1)}, u32[]{:S(2)}, u32[]{:S(2)}) collective-permute-start(bf16[64,8,512]{2,1,0:T(8,128)(2,1)S(1)} %get-tuple-element.36), channel_id=1, source_target_pairs={{1,0},{2,1},{3,2},{4,3},{5,4},{6,5},{7,6},{9,8},{10,9},{11,10},{12... | collective-permute-start | bytes 1572872 | tf_op jit(solution)/shard_map/ppermute | solution.py:29
  26.8 0.9 copy-start.3
  27.7 24.3 %all-to-all-start.1 = ((bf16[8,3,32,512]{3,2,1,0:T(8,128)(2,1)}), bf16[8,3,32,512]{3,2,1,0:T(8,128)(2,1)S(1)}, u32[]{:S(2)}, u32[]{:S(2)}) async-start(bf16[8,3,32,512]{3,2,1,0:T(8,128)(2,1)} %copy-done.3), calls=%async_computation.1 | async-start | bytes 1572864 | tf_op jit(solution)/shard_map/all_to_all | solution.py:475
  33.6 0.9 copy-start.2
  34.5 0.8 copy-start.4
  52.1 23.1 %all-to-all-start.2 = ((bf16[8,3,32,512]{3,2,1,0:T(8,128)(2,1)}), bf16[8,3,32,512]{3,2,1,0:T(8,128)(2,1)S(1)}, u32[]{:S(2)}, u32[]{:S(2)}) async-start(bf16[8,3,32,512]{3,2,1,0:T(8,128)(2,1)} %copy-done.2), calls=%async_computation.2 | async-start | bytes 1572864 | tf_op jit(solution)/shard_map/all_to_all | solution.py:475
  55.7 2.4 %collective-permute-start.4 = (bf16[8,3,32,512]{3,2,1,0:T(8,128)(2,1)S(1)}, bf16[8,3,32,512]{3,2,1,0:T(8,128)(2,1)S(1)}, u32[]{:S(2)}, u32[]{:S(2)}) collective-permute-start(bf16[8,3,32,512]{3,2,1,0:T(8,128)(2,1)S(1)} %after.5.own.rest_0_), channel_id=1, source_target_pairs={{0,8},{8,0},{16,24},{24,16},{1,9},{9,1},{17,25},{25,17},{2,10},{10... | collective-permute-start | bytes 2359304 | tf_op jit(solution)/shard_map/ppermute | solution.py:438
  55.8 20.1 %collective-permute-start.2 = (bf16[8,3,32,512]{3,2,1,0:T(8,128)(2,1)S(1)}, bf16[8,3,32,512]{3,2,1,0:T(8,128)(2,1)}, u32[]{:S(2)}, u32[]{:S(2)}) collective-permute-start(bf16[8,3,32,512]{3,2,1,0:T(8,128)(2,1)S(1)} %after.5.own.rest_0_), channel_id=1, source_target_pairs={{0,16},{8,24},{16,0},{24,8},{1,17},{9,25},{17,1},{25,9},{2,18},{10... | collective-permute-start | bytes 2359304 | tf_op jit(solution)/shard_map/ppermute | solution.py:438
  62.2 1.2 %copy-start = (bf16[3,1024,256]{2,1,0:T(8,128)(2,1)}, bf16[3,1024,256]{2,1,0:T(8,128)(2,1)S(1)}, u32[]{:S(2)}) copy-start(bf16[3,1024,256]{2,1,0:T(8,128)(2,1)S(1)} %left_sides.3.left.rest_2_) | copy-start | bytes 4718596
  75.2 8.8 %collective-permute-start.5 = (bf16[8,3,32,512]{3,2,1,0:T(8,128)(2,1)S(1)}, bf16[8,3,32,512]{3,2,1,0:T(8,128)(2,1)}, u32[]{:S(2)}, u32[]{:S(2)}) collective-permute-start(bf16[8,3,32,512]{3,2,1,0:T(8,128)(2,1)S(1)} %after.6.own.rest_0_), channel_id=1, source_target_pairs={{0,8},{8,0},{16,24},{24,16},{1,9},{9,1},{17,25},{25,17},{2,10},{10... | collective-permute-start | bytes 2359304 | tf_op jit(solution)/shard_map/ppermute | solution.py:438
  75.8 13.3 %collective-permute-start.3 = (bf16[8,3,32,512]{3,2,1,0:T(8,128)(2,1)}, bf16[8,3,32,512]{3,2,1,0:T(8,128)(2,1)}, u32[]{:S(2)}, u32[]{:S(2)}) collective-permute-start(bf16[8,3,32,512]{3,2,1,0:T(8,128)(2,1)} %collective-permute-done.2.rest_0_), channel_id=1, source_target_pairs={{0,8},{8,0},{16,24},{24,16},{1,9},{9,1},{17,25},{25,17},{2,10},{10... | collective-permute-start | bytes 2359304 | tf_op jit(solution)/shard_map/ppermute | solution.py:438
  75.8 20.1 %collective-permute-start.7 = (bf16[8,3,32,512]{3,2,1,0:T(8,128)(2,1)S(1)}, bf16[8,3,32,512]{3,2,1,0:T(8,128)(2,1)}, u32[]{:S(2)}, u32[]{:S(2)}) collective-permute-start(bf16[8,3,32,512]{3,2,1,0:T(8,128)(2,1)S(1)} %after.6.own.rest_0_), channel_id=1, source_target_pairs={{0,16},{8,24},{16,0},{24,8},{1,17},{9,25},{17,1},{25,9},{2,18},{10... | collective-permute-start | bytes 2359304 | tf_op jit(solution)/shard_map/ppermute | solution.py:438
  77.3 20.9 %all-to-all-start = ((bf16[8,2,32,512]{3,2,1,0:T(8,128)(2,1)}), bf16[8,2,32,512]{3,2,1,0:T(8,128)(2,1)S(1)}, u32[]{:S(2)}, u32[]{:S(2)}) async-start(bf16[8,2,32,512]{3,2,1,0:T(8,128)(2,1)} %copy-done.4), calls=%async_computation | async-start | bytes 1048576 | tf_op jit(solution)/shard_map/all_to_all | solution.py:475
  83.3 5.8 %copy-start.1 = (bf16[3,1024,256]{2,1,0:T(8,128)(2,1)S(1)}, bf16[3,1024,256]{2,1,0:T(8,128)(2,1)}, u32[]{:S(2)}) copy-start(bf16[3,1024,256]{2,1,0:T(8,128)(2,1)} %copy-done) | copy-start | bytes 4718596
  97.1 6.0 %collective-permute-start.8 = (bf16[8,3,32,512]{3,2,1,0:T(8,128)(2,1)S(1)}, bf16[8,3,32,512]{3,2,1,0:T(8,128)(2,1)}, u32[]{:S(2)}, u32[]{:S(2)}) collective-permute-start(bf16[8,3,32,512]{3,2,1,0:T(8,128)(2,1)S(1)} %after.8.rest_0_), channel_id=1, source_target_pairs={{0,8},{8,0},{16,24},{24,16},{1,9},{9,1},{17,25},{25,17},{2,10},{10... | collective-permute-start | bytes 2359304 | tf_op jit(solution)/shard_map/ppermute | solution.py:438
  98.2 2.0 %collective-permute-start.9 = (bf16[8,2,32,512]{3,2,1,0:T(8,128)(2,1)S(1)}, bf16[8,2,32,512]{3,2,1,0:T(8,128)(2,1)S(1)}, u32[]{:S(2)}, u32[]{:S(2)}) collective-permute-start(bf16[8,2,32,512]{3,2,1,0:T(8,128)(2,1)S(1)} %after.7.own.rest_0_), channel_id=1, source_target_pairs={{0,8},{8,0},{16,24},{24,16},{1,9},{9,1},{17,25},{25,17},{2,10},{10... | collective-permute-start | bytes 1572872 | tf_op jit(solution)/shard_map/ppermute | solution.py:438
  98.3 14.3 %collective-permute-start.6 = (bf16[8,2,32,512]{3,2,1,0:T(8,128)(2,1)S(1)}, bf16[8,2,32,512]{3,2,1,0:T(8,128)(2,1)S(1)}, u32[]{:S(2)}, u32[]{:S(2)}) collective-permute-start(bf16[8,2,32,512]{3,2,1,0:T(8,128)(2,1)S(1)} %after.7.own.rest_0_), channel_id=1, source_target_pairs={{0,16},{8,24},{16,0},{24,8},{1,17},{9,25},{17,1},{25,9},{2,18},{10... | collective-permute-start | bytes 1572872 | tf_op jit(solution)/shard_map/ppermute | solution.py:438
  112.6 2.0 %collective-permute-start.10 = (bf16[8,2,32,512]{3,2,1,0:T(8,128)(2,1)S(1)}, bf16[8,2,32,512]{3,2,1,0:T(8,128)(2,1)S(1)}, u32[]{:S(2)}, u32[]{:S(2)}) collective-permute-start(bf16[8,2,32,512]{3,2,1,0:T(8,128)(2,1)S(1)} %after.9.rest_0_), channel_id=1, source_target_pairs={{0,8},{8,0},{16,24},{24,16},{1,9},{9,1},{17,25},{25,17},{2,10},{10... | collective-permute-start | bytes 1572872 | tf_op jit(solution)/shard_map/ppermute | solution.py:438
